TPU v7x, 1024 devices: a whole 4x8x16 slice. The times are simulated.
1024 devices in a mesh: dp: 16 (over x, z_lo), shard: 64 (over z_hi, y, core).
Axes of the slice: x: 4, y: 8, z: 16 (z_hi: 4, z_lo: 4; z = z_hi * 4 + z_lo), core: 2. Of those that a mesh axis runs over, the one named last changes fastest.
Arguments:
- features: bfloat16 [2048, 4096], P('dp'), may hold values from -40 to 40
- out_grads: bfloat16 [2048, 16384], P('dp', 'shard'), may hold values from -120 to 120
- token_counts: int32 [16], replicated, may hold values from 42 to 128, as said below
- owner_order: int32 [32, 8], replicated, may hold values from 0 to 7, each once within a row
- moment: float32 [16384, 4096], P('shard', 'dp'), may hold values from -40 to 40
- second: float32 [16384, 4096], P('shard', 'dp'), may hold values from 0.03 to 1
- left_stat: float32 [64, 16, 128, 512], P('shard', 'dp'), may hold values from -0.5 to 2.5, as said below
- right_stat: float32 [64, 16, 128, 512], P('shard', 'dp'), may hold values from -0.5 to 2.5, as said below
- left_root: float32 [64, 16, 128, 512], P('shard', 'dp'), may hold values from -0.5 to 2, as said below
- right_root: float32 [64, 16, 128, 512], P('shard', 'dp'), may hold values from -0.5 to 2, as said below
Outputs:
- update: float32 [16384, 4096], P('shard', 'dp')
- new_moment: float32 [16384, 4096], P('shard', 'dp')
- new_second: float32 [16384, 4096], P('shard', 'dp')
- next_left: float32 [64, 16, 128, 512], P('shard', 'dp')
- next_right: float32 [64, 16, 128, 512], P('shard', 'dp')
Inputs may be any that keep to these rules, and one draw needn't show every extreme that they name: The first token_counts[g] tokens of group g are live, the others padding. `owner_order`: each row is a permutation of 0 to 7. `left_stat`: each block's matrix is symmetric. `right_stat`: each block's matrix is symmetric. `left_root`: each block's matrix is symmetric. `right_root`: each block's matrix is symmetric.
All inputs are finite; a program needn't handle non-finite values.
Results may differ from a plain program's by a relative error of at most 0.00035.
Values may be sent and summed in bfloat16 or wider, within the bound.
No kernel may reach another device: no remote copies, remote signals or barrier semaphores. Data moves between devices by JAX's collectives and lax.ppermute only.
A program may use at most 32 MiB of HBM per device.

v0:
```python
import jax
import jax.numpy as jnp
from jax import lax
from jax.sharding import PartitionSpec as P


def partner(value, axis, bit):
    return lax.ppermute(value, axis, [(i, i ^ 1 << bit) for i in range(lax.axis_size(axis))])


def stacked_rows(own_part, other_part, own_first):
    return jnp.where(
        own_first,
        jnp.concatenate([own_part, other_part], 0),
        jnp.concatenate([other_part, own_part], 0),
    )


def body(
    features,
    out_grads,
    token_counts,
    owner_order,
    moment,
    second,
    left_stat,
    right_stat,
    left_root,
    right_root,
):
    tok_rows = features.shape[0]
    block_size = left_stat.shape[-1]
    half_size = block_size // 2
    quarter = block_size // 4
    block_count = features.shape[1] // block_size
    row_index = lax.axis_index("dp")
    col_index = lax.axis_index("shard")
    side_bit = col_index % 2
    part_bit = row_index % 2
    exact = lax.Precision.HIGHEST
    token_total = jnp.sum(token_counts).astype(jnp.float32)
    live_rows = jnp.arange(tok_rows) < token_counts[row_index]
    masked = jnp.where(live_rows[:, None], out_grads, jnp.zeros_like(out_grads))
    block_perm = owner_order[col_index // 2]
    summed_rows = lax.psum_scatter(
        jnp.dot(masked.T, features, preferred_element_type=jnp.float32),
        "dp",
        scatter_dimension=0,
        tiled=True,
    )
    reordered = jnp.take(
        summed_rows.reshape(summed_rows.shape[0], block_count, block_size), block_perm, axis=1
    )
    outgoing = jnp.repeat(jnp.transpose(reordered, (1, 0, 2)), 2, axis=0)
    arrived = lax.all_to_all(outgoing, "dp", split_axis=0, concat_axis=1, tiled=True)
    own_half = arrived[0] / token_total
    left_mine = left_root[0, 0]
    right_mine = right_root[0, 0]
    other_half, other_right = partner((own_half, right_mine), "shard", 0)
    other_left = partner(left_mine, "dp", 0)
    whole_block = stacked_rows(own_half, other_half, side_bit == 0)
    left_rows_root = stacked_rows(left_mine, other_left, part_bit == 0)
    right_rows_root = stacked_rows(right_mine, other_right, side_bit == 0)
    left_rows = lax.dynamic_slice_in_dim(own_half, part_bit * quarter, quarter, 0)
    right_cols = lax.dynamic_slice_in_dim(
        whole_block, part_bit * half_size + side_bit * quarter, quarter, 1
    )
    next_left = 0.95 * left_stat[0, 0] + 0.05 * (
        jnp.dot(left_rows, whole_block.T, precision=exact) / block_size
    )
    next_right = 0.95 * right_stat[0, 0] + 0.05 * (
        jnp.dot(right_cols.T, whole_block, precision=exact) / block_size
    )
    tile_grad = lax.dynamic_slice_in_dim(own_half, part_bit * half_size, half_size, 1)
    new_moment = 0.9 * moment + 0.1 * tile_grad
    new_second = 0.95 * second + 0.05 * tile_grad * tile_grad
    direction = new_moment / (jnp.sqrt(new_second) + 1e-08)
    inner_left = jnp.dot(left_rows_root, whole_block, precision=exact)
    precond = jnp.dot(inner_left, right_rows_root.T, precision=exact)
    graft_totals = lax.psum(
        (jnp.sum(direction * direction), jnp.sum(precond * precond)), ("dp", "shard")
    )
    graft_scale = jnp.sqrt(graft_totals[0] / (graft_totals[1] + 1e-06))
    return (
        graft_scale * precond,
        new_moment,
        new_second,
        next_left[None, None],
        next_right[None, None],
    )


def solution(mesh):
    return jax.shard_map(
        body,
        mesh=mesh,
        in_specs=(
            P("dp", None),
            P("dp", "shard"),
            P(),
            P(),
            P("shard", "dp"),
            P("shard", "dp"),
            P("shard", "dp", None, None),
            P("shard", "dp", None, None),
            P("shard", "dp", None, None),
            P("shard", "dp", None, None),
        ),
        out_specs=(
            P("shard", "dp"),
            P("shard", "dp"),
            P("shard", "dp"),
            P("shard", "dp", None, None),
            P("shard", "dp", None, None),
        ),
        check_vma=False,
    )
```

profile of v0, /device:TPU:1, one launch (start us, length us, event | category | flops | bytes accessed | tf_op | source)
XLA Modules:
  0.0 308.9 jit_solution(2292901410705942471)
XLA Ops:
  7.2 0.0 copy-start
  7.2 0.0 reduce-scatter.2.cloned.1.call-start
  7.2 1.3 dynamic_slice.16
  8.6 0.6 iota_compare_fusion
  9.2 0.0 copy-done
  9.2 0.0 copy-start.4
  9.2 3.6 %fusion.21 = f32[256,4096]{1,0:T(8,128)} fusion(bf16[128,4096]{1,0:T(8,128)(2,1)S(1)} %copy-done, bf16[128,256]{1,0:T(8,128)(2,1)} %param.11, pred[128]{0:T(512)(128)(4,1)S(1)} %iota_compare_fusion), kind=kOutput, calls=%fused_computation.35 | convolution fusion | flops 268468224 | bytes 5308544 | tf_op jit(solution)/shard_map/dot_general | solution.py:46
  12.8 0.0 reduce-scatter.2.cloned.1.call-update
  12.9 0.2 dynamic-slice_reduce_fusion
  13.1 116.2 %reduce-scatter.2.cloned.1.call-done = f32[16,4096]{1,0:T(8,128)} async-done(((f32[256,4096]{1,0:T(8,128)}), f32[16,4096]{1,0:T(8,128)}) %reduce-scatter.2.cloned.1.call-update) | async-done | bytes 262160 | tf_op jit(solution)/shard_map/reduce_scatter | solution.py:45
  129.2 1.0 copy.19
  130.2 0.6 gather_fusion
  130.8 0.1 broadcast_select_fusion
  130.9 0.8 broadcast_in_dim.35
  131.7 5.2 %all-to-all-start = ((f32[16,16,512]{2,1,0:T(8,128)}), f32[16,16,512]{2,1,0:T(8,128)S(1)}, u32[]{:S(2)}, u32[]{:S(2)}) async-start(f32[16,16,512]{2,1,0:T(8,128)} %bitcast.2), calls=%async_computation.1 | async-start | bytes 1048576 | tf_op jit(solution)/shard_map/all_to_all | solution.py:55
  136.9 0.6 reduce_sum.27
  138.2 11.9 %all-to-all-done = f32[16,16,512]{2,1,0:T(8,128)S(1)} async-done(((f32[16,16,512]{2,1,0:T(8,128)}), f32[16,16,512]{2,1,0:T(8,128)S(1)}, u32[]{:S(2)}, u32[]{:S(2)}) %all-to-all-start) | async-done | bytes 524320 | tf_op jit(solution)/shard_map/all_to_all | solution.py:55
  150.1 0.1 broadcast_divide_fusion
  150.1 6.2 %collective-permute-start.1 = (f32[256,512]{1,0:T(8,128)S(1)}, f32[256,512]{1,0:T(8,128)S(1)}, u32[]{:S(2)}, u32[]{:S(2)}) collective-permute-start(f32[256,512]{1,0:T(8,128)S(1)} %bitcast.26), channel_id=1, source_target_pairs={{0,1},{1,0},{2,3},{3,2},{4,5},{5,4},{6,7},{7,6},{8,9},{9,8},{10,11... | collective-permute-start | bytes 1572872 | tf_op jit(solution)/shard_map/ppermute | solution.py:8
  156.4 1.9 collective-permute-start
  158.3 1.9 collective-permute-start.2
  160.3 1.5 multiply_reduce_fusion.1
  161.8 0.0 collective-permute-done.1
  161.8 0.1 maximum_select_fusion
  162.0 4.3 %collective-permute-done = f32[128,512]{1,0:T(8,128)} collective-permute-done((f32[128,512]{1,0:T(8,128)S(1)}, f32[128,512]{1,0:T(8,128)}, u32[]{:S(2)}, u32[]{:S(2)}) %collective-permute-start) | collective-permute-done | bytes 262176 | tf_op jit(solution)/shard_map/ppermute | solution.py:8
  166.3 2.1 fusion.4
  168.4 0.0 collective-permute-done.2
  168.4 2.4 multiply_reduce_fusion
  170.8 123.9 %all-reduce = (f32[]{:T(128)}, f32[]{:T(128)}) all-reduce(f32[]{:T(128)} %get-tuple-element.7, f32[]{:T(128)} %get-tuple-element.10), channel_id=1, replica_groups=mesh['dp'=16,'shard'=64] {'dp','shard'}, use_global_device_ids=true, to_apply=%region_3.4 | all-reduce | flops 2 | bytes 16 | tf_op jit(solution)/shard_map/psum | solution.py:80
  296.1 0.7 broadcast_multiply_fusion
  296.8 2.8 fusion.3
  299.6 2.5 fusion.1
  (12 shorter events, 0.0 us)
Async XLA Ops:
  7.2 2.0 copy-start
  7.2 122.1 %reduce-scatter.2.cloned.1.call-start = ((), (), s32[]{:S(2)}) async-start(), calls=%async_computation.2 | async-start | bytes 4456448 | tf_op jit(solution)/shard_map/reduce_scatter | solution.py:45
  9.2 3.6 %copy-start.4 = (s32[32,8]{0,1:T(8,128)S(1)}, s32[32,8]{0,1:T(8,128)}, u32[]{:S(2)}) copy-start(s32[32,8]{0,1:T(8,128)} %param.13) | copy-start | bytes 3076
  12.8 124.1 %copy-start.5 = (s32[16]{0:T(128)S(1)}, s32[16]{0:T(128)}, u32[]{:S(2)}) copy-start(s32[16]{0:T(128)} %param.12) | copy-start | bytes 196
  12.8 143.6 %copy-start.1 = (f32[1,1,128,512]{3,2,1,0:T(8,128)S(1)}, f32[1,1,128,512]{3,2,1,0:T(8,128)}, u32[]{:S(2)}) copy-start(f32[1,1,128,512]{3,2,1,0:T(8,128)} %param.18) | copy-start | bytes 786436
  12.8 147.5 %copy-start.2 = (f32[256,256]{1,0:T(8,128)S(1)}, f32[256,256]{1,0:T(8,128)}, u32[]{:S(2)}) copy-start(f32[256,256]{1,0:T(8,128)} %param.15) | copy-start | bytes 786436
  12.8 147.5 %copy-start.3 = (f32[256,256]{1,0:T(8,128)S(1)}, f32[256,256]{1,0:T(8,128)}, u32[]{:S(2)}) copy-start(f32[256,256]{1,0:T(8,128)} %param.14) | copy-start | bytes 786436
  131.7 18.3 %all-to-all-start = ((f32[16,16,512]{2,1,0:T(8,128)}), f32[16,16,512]{2,1,0:T(8,128)S(1)}, u32[]{:S(2)}, u32[]{:S(2)}) async-start(f32[16,16,512]{2,1,0:T(8,128)} %bitcast.2), calls=%async_computation.1 | async-start | bytes 1048576 | tf_op jit(solution)/shard_map/all_to_all | solution.py:55
  150.1 11.7 %collective-permute-start.1 = (f32[256,512]{1,0:T(8,128)S(1)}, f32[256,512]{1,0:T(8,128)S(1)}, u32[]{:S(2)}, u32[]{:S(2)}) collective-permute-start(f32[256,512]{1,0:T(8,128)S(1)} %bitcast.26), channel_id=1, source_target_pairs={{0,1},{1,0},{2,3},{3,2},{4,5},{5,4},{6,7},{7,6},{8,9},{9,8},{10,11... | collective-permute-start | bytes 1572872 | tf_op jit(solution)/shard_map/ppermute | solution.py:8
  156.4 9.9 %collective-permute-start = (f32[128,512]{1,0:T(8,128)S(1)}, f32[128,512]{1,0:T(8,128)}, u32[]{:S(2)}, u32[]{:S(2)}) collective-permute-start(f32[128,512]{1,0:T(8,128)S(1)} %bitcast.31), channel_id=1, source_target_pairs={{0,64},{64,0},{128,192},{192,128},{256,320},{320,256},{384,448},{4... | collective-permute-start | bytes 786440 | tf_op jit(solution)/shard_map/ppermute | solution.py:8
  158.3 10.1 %collective-permute-start.2 = (f32[128,512]{1,0:T(8,128)}, f32[128,512]{1,0:T(8,128)}, u32[]{:S(2)}, u32[]{:S(2)}) collective-permute-start(f32[128,512]{1,0:T(8,128)} %bitcast.34), channel_id=1, source_target_pairs={{0,1},{1,0},{2,3},{3,2},{4,5},{5,4},{6,7},{7,6},{8,9},{9,8},{10,11... | collective-permute-start | bytes 786440 | tf_op jit(solution)/shard_map/ppermute | solution.py:8
Sparse Core Ops, SparseCore 0:
  13.0 116.2 reduce-scatter.1
where the time goes:
time: 310 us; the launch traced here: 309 us
  waiting for transfers between devices  132 us (43%)
  blocking collectives  124 us (40%)
  between operations  16.3 us (5%)
  starting transfers between devices  15.3 us (5%)
  matrix products  13.4 us (4%)
  local copies, waits for them, and re-layouts  3.92 us (1%)
  other arithmetic  3.83 us (1%)
    psum x1, blocking collectives, body(): lax.psum((jnp.sum(direction * direction), jnp.sum(precond * precond)), ('...  124 us
    reduce_scatter x1, waiting for transfers between devices, body(): lax.psum_scatter(jnp.dot(masked.T, features, preferred_element_type=jnp.f...  116 us
    all_to_all x1, waiting for transfers between devices, body(): lax.all_to_all(outgoing, 'dp', split_axis=0, concat_axis=1, tiled=True)  11.9 us
    ppermute x3, starting transfers between devices, partner(): lax.ppermute(value, axis, [(i, i ^ 1 << bit) for i in range(lax.axis_size...  10.1 us
  transfers between devices with their start and end apart: 5, of which 3 were waited for; matrix products, arithmetic and copies ran while one was open for 1% of the time, Pallas kernels for 0%

commit v1 on v0

v1 whole, which is shorter than its diff:
```python
import jax
import jax.numpy as jnp
from jax import lax
from jax.sharding import Mesh, PartitionSpec as P

DP = ("x", "zl")
SHARD = ("zh", "y", "c")
SIZES = (4, 4, 4, 8, 2)


def partner(value, axis, bit=0):
    return lax.ppermute(value, axis, [(i, i ^ 1 << bit) for i in range(lax.axis_size(axis))])


def stacked_rows(own_part, other_part, own_first):
    return jnp.where(
        own_first,
        jnp.concatenate([own_part, other_part], 0),
        jnp.concatenate([other_part, own_part], 0),
    )


def total_over_devices(values):
    tile = jnp.concatenate([jnp.full((4, 128), v, jnp.float32) for v in values], 0)
    tile = tile + partner(tile, "c")
    for axes in (("x", "y"), ("zh", "zl")):
        copies = jnp.broadcast_to(tile, (lax.axis_size(axes), *tile.shape))
        tile = jnp.sum(lax.all_to_all(copies, axes, split_axis=0, concat_axis=0, tiled=True), 0)
    return tile[0, 0], tile[4, 0]


def body(
    features,
    out_grads,
    token_counts,
    owner_order,
    moment,
    second,
    left_stat,
    right_stat,
    left_root,
    right_root,
):
    tok_rows = features.shape[0]
    half_rows = tok_rows // 2
    block_size = left_stat.shape[-1]
    half_size = block_size // 2
    quarter = block_size // 4
    block_count = features.shape[1] // block_size
    row_index = lax.axis_index(DP)
    side_bit = lax.axis_index("c")
    part_bit = lax.axis_index("zl") % 2
    precise = lax.Precision.HIGH
    token_total = jnp.sum(token_counts).astype(jnp.float32)
    block_perm = owner_order[lax.axis_index(("zh", "y"))]
    left_mine = left_root[0, 0]
    right_mine = right_root[0, 0]

    live_rows = jnp.arange(tok_rows) < token_counts[row_index]
    masked = jnp.where(live_rows[:, None], out_grads, jnp.zeros_like(out_grads))
    kept = lax.dynamic_slice_in_dim(masked, side_bit * half_rows, half_rows, 0)
    given = lax.dynamic_slice_in_dim(masked, (1 - side_bit) * half_rows, half_rows, 0)
    taken = partner(given, "c")
    own_first = side_bit == 0
    grads_half = jnp.where(
        own_first,
        jnp.concatenate([kept, taken], 1),
        jnp.concatenate([taken, kept], 1),
    )
    feats_half = lax.dynamic_slice_in_dim(features, side_bit * half_rows, half_rows, 0)
    blocks = [
        lax.dynamic_slice_in_dim(feats_half, block_perm[k] * block_size, block_size, 1)
        for k in range(block_count)
    ]
    outgoing = jnp.stack(
        [jnp.concatenate([blocks[k // 2], grads_half], 1) for k in range(2 * block_count)], 0
    )
    arrived = lax.all_to_all(outgoing, DP, split_axis=0, concat_axis=0, tiled=True)
    arrived = arrived.reshape(-1, 2 * block_size)
    partial = jnp.dot(
        arrived[:, block_size:].T, arrived[:, :block_size], preferred_element_type=jnp.float32
    )
    other_left = partner(left_mine, "zl")
    other_right = partner(right_mine, "c")
    whole_block = (partial + partner(partial, "c")) / token_total

    left_rows_root = stacked_rows(left_mine, other_left, part_bit == 0)
    right_rows_root = stacked_rows(right_mine, other_right, own_first)
    own_half = lax.dynamic_slice_in_dim(whole_block, side_bit * half_size, half_size, 0)
    left_rows = lax.dynamic_slice_in_dim(own_half, part_bit * quarter, quarter, 0)
    right_cols = lax.dynamic_slice_in_dim(
        whole_block, part_bit * half_size + side_bit * quarter, quarter, 1
    )
    tile_grad = lax.dynamic_slice_in_dim(own_half, part_bit * half_size, half_size, 1)
    new_moment = 0.9 * moment + 0.1 * tile_grad
    new_second = 0.95 * second + 0.05 * tile_grad * tile_grad
    direction = new_moment / (jnp.sqrt(new_second) + 1e-08)
    inner_left = jnp.dot(left_rows_root, whole_block, precision=precise)
    precond = jnp.dot(inner_left, right_rows_root.T, precision=precise)
    graft_totals = total_over_devices(
        (jnp.sum(direction * direction), jnp.sum(precond * precond))
    )
    next_left = 0.95 * left_stat[0, 0] + 0.05 * (
        jnp.dot(left_rows, whole_block.T, precision=precise) / block_size
    )
    next_right = 0.95 * right_stat[0, 0] + 0.05 * (
        jnp.dot(right_cols.T, whole_block, precision=precise) / block_size
    )
    graft_scale = jnp.sqrt(graft_totals[0] / (graft_totals[1] + 1e-06))
    return (
        graft_scale * precond,
        new_moment,
        new_second,
        next_left[None, None],
        next_right[None, None],
    )


def solution(mesh):
    fine = Mesh(mesh.devices.reshape(SIZES), DP + SHARD)
    return jax.shard_map(
        body,
        mesh=fine,
        in_specs=(
            P(DP, None),
            P(DP, SHARD),
            P(),
            P(),
            P(SHARD, DP),
            P(SHARD, DP),
            P(SHARD, DP, None, None),
            P(SHARD, DP, None, None),
            P(SHARD, DP, None, None),
            P(SHARD, DP, None, None),
        ),
        out_specs=(
            P(SHARD, DP),
            P(SHARD, DP),
            P(SHARD, DP),
            P(SHARD, DP, None, None),
            P(SHARD, DP, None, None),
        ),
        check_vma=False,
    )
```

time: 310 us -> 147 us (0.47)
  waiting for transfers between devices: 132 us -> 20.8 us
  blocking collectives: 124 us -> 52.7 us
  starting transfers between devices: 15.3 us -> 43 us
  between operations: 16.3 us -> 8.03 us
  matrix products: 13.4 us -> 7.31 us
    psum x1 -> x0, blocking collectives: 124 us -> none  [body(): lax.psum((jnp.sum(direction * direction), jnp.sum(precond * precond)), ('...]
    reduce_scatter x1 -> x0, waiting for transfers between devices: 116 us -> none  [body(): lax.psum_scatter(jnp.dot(masked.T, features, preferred_element_type=jnp.f...]
    all_to_all x0 -> x1, blocking collectives: none -> 52.7 us  [body(): lax.all_to_all(outgoing, DP, split_axis=0, concat_axis=0, tiled=True)]
    ppermute x3 -> x5, starting transfers between devices: 10.1 us -> 25.6 us  [partner(): lax.ppermute(value, axis, [(i, i ^ 1 << bit) for i in range(lax.axis_size...]
    all_to_all x1 -> x2, starting transfers between devices: 5.19 us -> 17.4 us  [total_over_devices(): lax.all_to_all(copies, axes, split_axis=0, concat_axis=0, tiled=True)]
    all_to_all x1 -> x2, waiting for transfers between devices: 11.9 us -> 18.1 us  [total_over_devices(): lax.all_to_all(copies, axes, split_axis=0, concat_axis=0, tiled=True)]
    dot_general x5, matrix products: 13.4 us -> 7.31 us  [the longest x1 2.26 us: body(): precond = jnp.dot(inner_left, right_rows_root.T, precision=precise)]
  transfers between devices with their start and end apart: 5 -> 7, of which waited for: 3 -> 4; matrix products, arithmetic and copies ran while one was open for 1% -> 7% of each run, Pallas kernels for 0% -> 0%
where the time goes in v1:
time: 147 us; the launch traced here: 145 us
  blocking collectives  52.7 us (36%)
  starting transfers between devices  43 us (29%)
  waiting for transfers between devices  20.8 us (14%)
  between operations  8.03 us (5%)
  matrix products  7.31 us (5%)
  local copies, waits for them, and re-layouts  6.72 us (5%)
  other arithmetic  6.12 us (4%)
    all_to_all x1, blocking collectives, body(): lax.all_to_all(outgoing, DP, split_axis=0, concat_axis=0, tiled=True)  52.7 us
    ppermute x5, starting transfers between devices, partner(): lax.ppermute(value, axis, [(i, i ^ 1 << bit) for i in range(lax.axis_size...  25.6 us
    all_to_all x2, waiting for transfers between devices, total_over_devices(): lax.all_to_all(copies, axes, split_axis=0, concat_axis=0, tiled=True)  18.1 us
    all_to_all x2, starting transfers between devices, total_over_devices(): lax.all_to_all(copies, axes, split_axis=0, concat_axis=0, tiled=True)  17.4 us
  transfers between devices with their start and end apart: 7, of which 4 were waited for; matrix products, arithmetic and copies ran while one was open for 7% of the time, Pallas kernels for 0%

profile of v1, /device:TPU:1, one launch (start us, length us, event | category | flops | bytes accessed | tf_op | source)
XLA Modules:
  0.0 144.7 jit_solution(2681836528926347925)
XLA Ops:
  0.7 1.2 dynamic_slice.52
  1.9 0.6 iota_compare_fusion
  2.6 0.9 broadcast_select_fusion
  3.5 16.1 %collective-permute-start = (bf16[64,256]{1,0:T(8,128)(2,1)S(1)}, bf16[64,256]{1,0:T(8,128)(2,1)S(1)}, u32[]{:S(2)}, u32[]{:S(2)}) collective-permute-start(bf16[64,256]{1,0:T(8,128)(2,1)S(1)} %get-tuple-element.17), channel_id=1, source_target_pairs={{0,1},{1,0},{2,3},{3,2},{4,5},{5,4},{6,7},{7,6},{8,9},{9,8},{10,11... | collective-permute-start | bytes 98312 | tf_op jit(solution)/shard_map/ppermute | solution.py:12
  19.6 0.1 constant_dynamic-slice_fusion.2
  19.7 0.6 fusion.55
  25.4 1.6 %fusion.53 = (bf16[64,512]{1,0:T(8,128)(2,1)S(1)}, bf16[64,512]{1,0:T(8,128)(2,1)S(1)}, bf16[64,512]{1,0:T(8,128)(2,1)S(1)}, bf16[64,512]{1,0:T(8,128)(2,1)S(1)}...) fusion(bf16[128,4096]{1,0:T(8,128)(2,1)} %param.10, ...), kind=kLoop, calls=%fused_computation.77 | loop fusion | bytes 1048612 | tf_op jit(solution)/shard_map/dynamic_slice | solution.py:72
  27.3 52.7 %all_to_all.15 = bf16[16,64,1024]{2,1,0:T(8,128)(2,1)S(1)} all-to-all(bf16[16,64,1024]{2,1,0:T(8,128)(2,1)S(1)} %fusion.33), channel_id=1, replica_groups=mesh['x'=4,'zl'=4,'zh'=4,'y'=8,'c'=2] {'x','zl'}, dimensions={0} | all-to-all | bytes 4194304 | tf_op jit(solution)/shard_map/all_to_all | solution.py:78
  80.0 0.7 fusion.4
  80.8 3.0 %collective-permute-start.1 = (f32[512,512]{1,0:T(8,128)S(1)}, f32[512,512]{1,0:T(8,128)S(1)}, u32[]{:S(2)}, u32[]{:S(2)}) collective-permute-start(f32[512,512]{1,0:T(8,128)S(1)} %fusion.4), channel_id=1, source_target_pairs={{0,1},{1,0},{2,3},{3,2},{4,5},{5,4},{6,7},{7,6},{8,9},{9,8},{10,11... | collective-permute-start | bytes 3145736 | tf_op jit(solution)/shard_map/ppermute | solution.py:12
  83.8 1.9 %collective-permute-start.2 = (f32[128,512]{1,0:T(8,128)S(1)}, f32[128,512]{1,0:T(8,128)}, u32[]{:S(2)}, u32[]{:S(2)}) collective-permute-start(f32[128,512]{1,0:T(8,128)S(1)} %bitcast.74), channel_id=1, source_target_pairs={{0,64},{64,0},{128,192},{192,128},{1,65},{65,1},{129,193},{193,129... | collective-permute-start | bytes 786440 | tf_op jit(solution)/shard_map/ppermute | solution.py:12
  85.7 1.9 %collective-permute-start.3 = (f32[128,512]{1,0:T(8,128)}, f32[128,512]{1,0:T(8,128)}, u32[]{:S(2)}, u32[]{:S(2)}) collective-permute-start(f32[128,512]{1,0:T(8,128)} %bitcast.19), channel_id=1, source_target_pairs={{0,1},{1,0},{2,3},{3,2},{4,5},{5,4},{6,7},{7,6},{8,9},{9,8},{10,11... | collective-permute-start | bytes 786440 | tf_op jit(solution)/shard_map/ppermute | solution.py:12
  87.7 0.6 reduce_sum.45
  89.0 0.2 add_divide_fusion
  89.2 2.6 %multiply_reduce_fusion.1 = (f32[]{:T(128)}, f32[256,256]{1,0:T(8,128)}, f32[256,256]{1,0:T(8,128)}) fusion(f32[512,512]{1,0:T(8,128)S(1)} %add_divide_fusion, s32[]{:T(128)S(6)} %select_n.131, s32[]{:T(128)S(6)} %select_n.134, f32[256,256]{1,0:T(8,128)} %param.15, f32[256,256]{1,0:T(8,128)} %param.14), kind=kLoop, calls=%fused_computation.29 | loop fusion | flops 720895 | bytes 1310732 | tf_op jit(solution)/shard_map/reduce_sum | solution.py:101
  91.9 1.9 %collective-permute-done.2 = f32[128,512]{1,0:T(8,128)} collective-permute-done((f32[128,512]{1,0:T(8,128)S(1)}, f32[128,512]{1,0:T(8,128)}, u32[]{:S(2)}, u32[]{:S(2)}) %collective-permute-start.2) | collective-permute-done | bytes 262176 | tf_op jit(solution)/shard_map/ppermute | solution.py:12
  93.7 1.7 %fusion.7 = f32[256,512]{1,0:T(8,128)S(1)} fusion(f32[512,512]{1,0:T(8,128)S(1)} %add_divide_fusion, f32[128,512]{1,0:T(8,128)} %collective-permute-done.2, f32[128,512]{1,0:T(8,128)S(1)} %bitcast.75, pred[]{:T(512)S(6)} %eq.9), kind=kOutput, calls=%fused_computation.11 | convolution fusion | flops 403046400 | bytes 2097153 | tf_op jit(solution)/shard_map/dot_general | solution.py:98
  95.5 2.3 %multiply_reduce_fusion = (f32[]{:T(128)}, f32[256,256]{1,0:T(8,128)S(1)}) fusion(f32[256,512]{1,0:T(8,128)S(1)} %fusion.7, f32[128,512]{1,0:T(8,128)} %collective-permute-done.3, f32[128,512]{1,0:T(8,128)} %bitcast.19, pred[]{:T(512)S(6)} %eq.8), kind=kOutput, calls=%fused_computation.28 | convolution fusion | flops 201850880 | bytes 1310725 | tf_op jit(solution)/shard_map/dot_general | solution.py:99
  97.7 0.6 broadcast_in_dim.30
  98.4 0.7 concatenate.69
  99.1 2.7 %collective-permute-start.4 = (f32[8,128]{1,0:T(8,128)S(1)}, f32[8,128]{1,0:T(8,128)S(1)}, u32[]{:S(2)}, u32[]{:S(2)}) collective-permute-start(f32[8,128]{1,0:T(8,128)S(1)} %concatenate.70), channel_id=1, source_target_pairs={{0,1},{1,0},{2,3},{3,2},{4,5},{5,4},{6,7},{7,6},{8,9},{9,8},{10,11... | collective-permute-start | bytes 12296 | tf_op jit(solution)/shard_map/ppermute | solution.py:12
  101.8 0.8 collective-permute-done.4
  102.7 0.7 broadcast_in_dim.31
  103.3 3.9 %all-to-all-start.1 = ((f32[32,8,128]{2,1,0:T(8,128)}), f32[32,8,128]{2,1,0:T(8,128)S(1)}, u32[]{:S(2)}, u32[]{:S(2)}) async-start(f32[32,8,128]{2,1,0:T(8,128)} %broadcast_in_dim.31), calls=%async_computation.1 | async-start | bytes 262144 | tf_op jit(solution)/shard_map/all_to_all | solution.py:28
  107.2 9.1 %all-to-all-done.1 = f32[32,8,128]{2,1,0:T(8,128)S(1)} async-done(((f32[32,8,128]{2,1,0:T(8,128)}), f32[32,8,128]{2,1,0:T(8,128)S(1)}, u32[]{:S(2)}, u32[]{:S(2)}) %all-to-all-start.1) | async-done | bytes 131104 | tf_op jit(solution)/shard_map/all_to_all | solution.py:28
  116.4 0.6 broadcast_in_dim.32
  117.0 13.5 %all-to-all-start.2 = ((f32[16,8,128]{2,1,0:T(8,128)}), f32[16,8,128]{2,1,0:T(8,128)S(1)}, u32[]{:S(2)}, u32[]{:S(2)}) async-start(f32[16,8,128]{2,1,0:T(8,128)} %broadcast_in_dim.32), calls=%async_computation.2 | async-start | bytes 131072 | tf_op jit(solution)/shard_map/all_to_all | solution.py:28
  130.6 1.4 fusion.3
  132.0 1.2 fusion.1
  133.2 9.0 %all-to-all-done.2 = f32[16,8,128]{2,1,0:T(8,128)S(1)} async-done(((f32[16,8,128]{2,1,0:T(8,128)}), f32[16,8,128]{2,1,0:T(8,128)S(1)}, u32[]{:S(2)}, u32[]{:S(2)}) %all-to-all-start.2) | async-done | bytes 65568 | tf_op jit(solution)/shard_map/all_to_all | solution.py:28
  142.2 0.5 fusion.54
  144.0 0.7 broadcast_multiply_fusion
  (35 shorter events, 0.4 us)
Async XLA Ops:
  0.6 19.0 %copy-start = (s32[32,8]{0,1:T(8,128)S(1)}, s32[32,8]{0,1:T(8,128)}, u32[]{:S(2)}) copy-start(s32[32,8]{0,1:T(8,128)} %param.13) | copy-start | bytes 3076
  3.5 23.4 %collective-permute-start = (bf16[64,256]{1,0:T(8,128)(2,1)S(1)}, bf16[64,256]{1,0:T(8,128)(2,1)S(1)}, u32[]{:S(2)}, u32[]{:S(2)}) collective-permute-start(bf16[64,256]{1,0:T(8,128)(2,1)S(1)} %get-tuple-element.17), channel_id=1, source_target_pairs={{0,1},{1,0},{2,3},{3,2},{4,5},{5,4},{6,7},{7,6},{8,9},{9,8},{10,11... | collective-permute-start | bytes 98312 | tf_op jit(solution)/shard_map/ppermute | solution.py:12
  80.0 3.8 %copy-start.1 = (f32[1,1,128,512]{3,2,1,0:T(8,128)S(1)}, f32[1,1,128,512]{3,2,1,0:T(8,128)}, u32[]{:S(2)}) copy-start(f32[1,1,128,512]{3,2,1,0:T(8,128)} %param.18) | copy-start | bytes 786436
  80.0 7.6 %copy-start.4 = (s32[16]{0:T(128)S(1)}, s32[16]{0:T(128)}, u32[]{:S(2)}) copy-start(s32[16]{0:T(128)} %param.12) | copy-start | bytes 196
  80.8 8.2 %collective-permute-start.1 = (f32[512,512]{1,0:T(8,128)S(1)}, f32[512,512]{1,0:T(8,128)S(1)}, u32[]{:S(2)}, u32[]{:S(2)}) collective-permute-start(f32[512,512]{1,0:T(8,128)S(1)} %fusion.4), channel_id=1, source_target_pairs={{0,1},{1,0},{2,3},{3,2},{4,5},{5,4},{6,7},{7,6},{8,9},{9,8},{10,11... | collective-permute-start | bytes 3145736 | tf_op jit(solution)/shard_map/ppermute | solution.py:12
  83.8 9.9 %collective-permute-start.2 = (f32[128,512]{1,0:T(8,128)S(1)}, f32[128,512]{1,0:T(8,128)}, u32[]{:S(2)}, u32[]{:S(2)}) collective-permute-start(f32[128,512]{1,0:T(8,128)S(1)} %bitcast.74), channel_id=1, source_target_pairs={{0,64},{64,0},{128,192},{192,128},{1,65},{65,1},{129,193},{193,129... | collective-permute-start | bytes 786440 | tf_op jit(solution)/shard_map/ppermute | solution.py:12
  85.7 9.7 %collective-permute-start.3 = (f32[128,512]{1,0:T(8,128)}, f32[128,512]{1,0:T(8,128)}, u32[]{:S(2)}, u32[]{:S(2)}) collective-permute-start(f32[128,512]{1,0:T(8,128)} %bitcast.19), channel_id=1, source_target_pairs={{0,1},{1,0},{2,3},{3,2},{4,5},{5,4},{6,7},{7,6},{8,9},{9,8},{10,11... | collective-permute-start | bytes 786440 | tf_op jit(solution)/shard_map/ppermute | solution.py:12
  91.9 38.7 %copy-start.2 = (f32[1,1,128,512]{3,2,1,0:T(8,128)S(1)}, f32[1,1,128,512]{3,2,1,0:T(8,128)}, u32[]{:S(2)}) copy-start(f32[1,1,128,512]{3,2,1,0:T(8,128)} %param.16) | copy-start | bytes 786436
  95.4 36.5 %copy-start.3 = (f32[1,1,128,512]{3,2,1,0:T(8,128)S(1)}, f32[1,1,128,512]{3,2,1,0:T(8,128)}, u32[]{:S(2)}) copy-start(f32[1,1,128,512]{3,2,1,0:T(8,128)} %param.17) | copy-start | bytes 786436
  99.1 3.5 %collective-permute-start.4 = (f32[8,128]{1,0:T(8,128)S(1)}, f32[8,128]{1,0:T(8,128)S(1)}, u32[]{:S(2)}, u32[]{:S(2)}) collective-permute-start(f32[8,128]{1,0:T(8,128)S(1)} %concatenate.70), channel_id=1, source_target_pairs={{0,1},{1,0},{2,3},{3,2},{4,5},{5,4},{6,7},{7,6},{8,9},{9,8},{10,11... | collective-permute-start | bytes 12296 | tf_op jit(solution)/shard_map/ppermute | solution.py:12
  103.3 13.0 %all-to-all-start.1 = ((f32[32,8,128]{2,1,0:T(8,128)}), f32[32,8,128]{2,1,0:T(8,128)S(1)}, u32[]{:S(2)}, u32[]{:S(2)}) async-start(f32[32,8,128]{2,1,0:T(8,128)} %broadcast_in_dim.31), calls=%async_computation.1 | async-start | bytes 262144 | tf_op jit(solution)/shard_map/all_to_all | solution.py:28
  117.0 25.2 %all-to-all-start.2 = ((f32[16,8,128]{2,1,0:T(8,128)}), f32[16,8,128]{2,1,0:T(8,128)S(1)}, u32[]{:S(2)}, u32[]{:S(2)}) async-start(f32[16,8,128]{2,1,0:T(8,128)} %broadcast_in_dim.32), calls=%async_computation.2 | async-start | bytes 131072 | tf_op jit(solution)/shard_map/all_to_all | solution.py:28
